TPU v7x, 256 devices: a whole 4x4x8 slice. The times are simulated.
256 devices in a mesh: mem: 4 (over y_lo, core), lat: 16 (over y_hi, z), lon: 4 (over x).
Axes of the slice: x: 4, y: 4 (y_hi: 2, y_lo: 2; y = y_hi * 2 + y_lo), z: 8, core: 2. Of those that a mesh axis runs over, the one named last changes fastest.
Arguments:
- anomalies: bfloat16 [64, 4, 384, 768], P('mem', None, 'lat', 'lon'), may hold values from -6 to 6
- innovation: float32 [1048576], P(('mem', 'lat', 'lon')), may hold values from -6 to 6
- corner_frac: float32 [2, 1048576], P(None, ('mem', 'lat', 'lon')), may hold values from 0 to 1
- corner_cell: int32 [1048576], P(('mem', 'lat', 'lon')), may hold values from 0 to 4414, as said below
- cell_owner: int32 [1048576], P(('mem', 'lat', 'lon')), may hold values from 0 to 63, as said below
- latitude_kernel: bfloat16 [384, 384], replicated, as said below
- longitude_kernel: bfloat16 [768, 768], replicated, as said below
Outputs:
- gradient: bfloat16 [64, 4, 384, 768], P('mem', None, 'lat', 'lon')
Inputs may be any that keep to these rules, and one draw needn't show every extreme that they name: corner_cell = r * 192 + c with r < 23 and c < 191, so all four corners lie in the tile. `cell_owner`: tile t is latitude band t // 4 and longitude part t % 4. The observations of one device name each tile at most 256 times; between 1 and 4 tiles exactly 256 times, one of them the same tile for every device; the other tiles' counts on that device differ by at most one. `latitude_kernel`: nonnegative. `longitude_kernel`: nonnegative.
All inputs are finite; a program needn't handle non-finite values.
Results may differ from a plain program's by a relative error of at most 0.0057.
Values may be sent and summed in bfloat16 or wider, within the bound.
A program may use at most 128 MiB of HBM per device.

v0:
```python
import jax
import jax.numpy as jnp
from jax import lax
from jax.sharding import PartitionSpec as P


def spread_grid(values, frac_row, frac_col, cell_index, row_count, row_width):
    slot_total = values.shape[0]
    block_size = min(2048, slot_total)
    block_count = slot_total // block_size
    row_ids = jnp.arange(row_count, dtype=jnp.int32)
    col_ids = jnp.arange(row_width, dtype=jnp.int32)

    def add_block(block, grid_sum):
        start = block * block_size
        value_part = lax.dynamic_slice_in_dim(values, start, block_size)
        row_frac = lax.dynamic_slice_in_dim(frac_row, start, block_size)
        col_frac = lax.dynamic_slice_in_dim(frac_col, start, block_size)
        cell_part = lax.dynamic_slice_in_dim(cell_index, start, block_size)
        cell_row = cell_part // row_width
        cell_col = cell_part % row_width
        row_table = jnp.where(row_ids[None, :] == cell_row[:, None], 1.0 - row_frac[:, None], 0.0)
        row_table = row_table + jnp.where(
            row_ids[None, :] == cell_row[:, None] + 1, row_frac[:, None], 0.0
        )
        col_table = jnp.where(col_ids[None, :] == cell_col[:, None], 1.0 - col_frac[:, None], 0.0)
        col_table = col_table + jnp.where(
            col_ids[None, :] == cell_col[:, None] + 1, col_frac[:, None], 0.0
        )
        row_table = row_table * value_part[:, None]
        return grid_sum + jnp.dot(
            row_table.T,
            col_table,
            precision=lax.Precision.HIGHEST,
            preferred_element_type=jnp.float32,
        )

    return lax.fori_loop(0, block_count, add_block, jnp.zeros((row_count, row_width), jnp.float32))


def deliver(values, fractions, cell_index, owners, tile_count, row_count, row_width):
    count_obs = owners.shape[0]
    capacity = 4 * count_obs // tile_count
    tile_ids = jnp.arange(tile_count, dtype=jnp.int32)
    one_hot = (owners[:, None] == tile_ids[None, :]).astype(jnp.int32)
    running = jnp.cumsum(one_hot, axis=0) - one_hot
    rank_index = jnp.sum(running * one_hot, axis=1)
    slot_index = owners * capacity + rank_index
    payload = jnp.stack([values, fractions[0], fractions[1]], axis=1)
    placed = jnp.zeros((tile_count * capacity, 3), jnp.float32).at[slot_index].set(payload)
    floats = placed.reshape(tile_count, capacity, 3).transpose(0, 2, 1)
    integers = (
        jnp.zeros((tile_count * capacity,), jnp.int32)
        .at[slot_index]
        .set(cell_index)
        .reshape(tile_count, capacity)
    )
    got_floats, got_cells = (
        lax.all_to_all(floats, ("lat", "lon"), split_axis=0, concat_axis=0, tiled=True),
        lax.all_to_all(integers, ("lat", "lon"), split_axis=0, concat_axis=0, tiled=True),
    )
    return spread_grid(
        got_floats[:, 0, :].reshape(-1),
        got_floats[:, 1, :].reshape(-1),
        got_floats[:, 2, :].reshape(-1),
        got_cells.reshape(-1),
        row_count,
        row_width,
    )


def shards(
    anomalies, innovation, corner_frac, corner_cell, cell_owner, latitude_kernel, longitude_kernel
):
    row_count = anomalies.shape[2]
    col_count = anomalies.shape[3]
    tile_count = lax.axis_size("lat") * lax.axis_size("lon")
    partial_grid = deliver(
        innovation, corner_frac, corner_cell, cell_owner, tile_count, row_count, col_count
    )
    forcing = lax.psum(partial_grid, "mem")
    weighted = (anomalies.astype(jnp.float32) * forcing).astype(jnp.bfloat16)
    mixed = jnp.einsum(
        "il,mkij->mklj",
        latitude_kernel,
        lax.all_to_all(weighted, "lat", split_axis=0, concat_axis=2, tiled=True),
        preferred_element_type=jnp.float32,
    ).astype(jnp.bfloat16)
    after_rows = lax.all_to_all(mixed, "lat", split_axis=2, concat_axis=0, tiled=True)
    product = jnp.einsum(
        "mklj,jp->mklp",
        lax.all_to_all(after_rows, "lon", split_axis=0, concat_axis=3, tiled=True),
        longitude_kernel,
        preferred_element_type=jnp.float32,
    ).astype(jnp.bfloat16)
    return lax.all_to_all(product, "lon", split_axis=3, concat_axis=0, tiled=True)


def solution(mesh):
    placed = (
        P("mem", None, "lat", "lon"),
        P(("mem", "lat", "lon")),
        P(None, ("mem", "lat", "lon")),
        P(("mem", "lat", "lon")),
        P(("mem", "lat", "lon")),
        P(),
        P(),
    )
    return jax.shard_map(
        shards, mesh=mesh, in_specs=placed, out_specs=P("mem", None, "lat", "lon"), check_vma=False
    )
```

profile of v0, /device:TPU:16, one launch (start us, length us, event | category | flops | bytes accessed | tf_op | source)
XLA Modules:
  0.0 242.7 jit_solution(9820558987967508071)
XLA Ops:
  0.0 0.9 fusion.35
  0.9 18.4 %reduce-window.6 = s32[64,32,128]{2,1,0:T(8,128)S(1)} reduce-window(s32[64,32,128]{2,1,0:T(8,128)S(1)} %fusion.35, s32[]{:T(128)} %constant.99.clone.1), window={size=1x1x128 pad=0_0x0_0x127_0}, to_apply=%region_0.0 | reduce-window | flops 33292288 | bytes 2097156 | tf_op jit(solution)/shard_map/reduce-window
  20.8 0.9 fusion.34
  21.8 0.6 copy.29
  22.4 14.3 %scatter_custom_fusion.1 = f32[16384,3]{1,0:T(8,128)} fusion(s32[4096]{0:T(1024)S(1)} %compare_select_fusion, f32[4096,3]{1,0:T(8,128)S(1)} %copy.29, f32[]{:T(128)} %constant.100.clone.1), kind=kCustom, calls=%fused_computation.38 | custom fusion | bytes 196612 | tf_op jit(solution)/shard_map/scatter | solution.py:50
  36.7 5.9 %copy.30 = f32[64,256,3]{1,2,0:T(4,128)} copy(f32[64,256,3]{2,1,0:T(8,128)} %bitcast.66) | data formatting | bytes 393216 | tf_op jit(solution)/shard_map/reshape | solution.py:51
  42.7 14.5 %all-to-all-start.1 = ((f32[64,3,256]{2,1,0:T(4,128)}), f32[64,3,256]{2,1,0:T(4,128)S(1)}, u32[]{:S(2)}, u32[]{:S(2)}) async-start(f32[64,3,256]{2,1,0:T(4,128)} %bitcast.10), calls=%async_computation.1 | async-start | bytes 524288 | tf_op jit(solution)/shard_map/all_to_all | solution.py:59
  57.2 16.3 %scatter_custom_fusion = s32[16384]{0:T(1024)} fusion(s32[4096]{0:T(1024)S(1)} %compare_select_fusion, s32[4096]{0:T(1024)} %param.12, s32[]{:T(128)} %constant.99.clone.1), kind=kCustom, calls=%fused_computation.57 | custom fusion | bytes 66048 | tf_op jit(solution)/shard_map/scatter | solution.py:55
  73.5 12.8 %all-to-all-start = ((s32[64,1,256]{2,1,0:T(1,128)}), s32[64,1,256]{2,1,0:T(1,128)S(1)}, u32[]{:S(2)}, u32[]{:S(2)}) async-start(s32[64,1,256]{2,1,0:T(1,128)} %bitcast.4), calls=%async_computation | async-start | bytes 131072 | tf_op jit(solution)/shard_map/all_to_all | solution.py:60
  86.5 9.3 %all-to-all-done = s32[64,1,256]{2,1,0:T(1,128)S(1)} async-done(((s32[64,1,256]{2,1,0:T(1,128)}), s32[64,1,256]{2,1,0:T(1,128)S(1)}, u32[]{:S(2)}, u32[]{:S(2)}) %all-to-all-start) | async-done | bytes 65568 | tf_op jit(solution)/shard_map/all_to_all | solution.py:60
  95.7 35.3 %while.17 = (s32[]{:T(128)}, f32[24,192]{1,0:T(8,128)S(1)}, s32[16384]{0:T(1024)S(1)}, f32[16384]{0:T(1024)S(1)}, f32[16384]{0:T(1024)S(1)}, /*index=5*/f32[1638...) while((s32[]{:T(128)}, f32[24,192]{1,0:T(8,128)S(1)}, s32[16384]{0:T(1024)S(1)}, ...), condition=%wide.region_6.7_spmd.clone.clone, body=%wide.region_5.6_spmd.clone.clone.sunk | while | flops 115549192 | bytes 217257 | solution.py:38
  95.8 4.3 %fusion.47 = f32[24,192]{1,0:T(8,128)S(1)} fusion(f32[2048]{0:T(1024)S(1)} %get-tuple-element.335, s32[2048]{0:T(1024)S(1)} %get-tuple-element.336, f32[2048]{0:T(1024)S(1)} %get-tuple-element.337, s32[2048]{0:T(1024)S(1)} %get-tuple-element.338, f32[2048]{0:T(1024)S(1)} %dynamic_slice.57, f32[2048]{0:T(1024)S(1)} %get-tuple-element.339, ...), kind=kOutput, calls=%fused_computation.12.clone.1 | convolution fusion | flops 115516416 | bytes 110593 | tf_op jit(solution)/shard_map/while/body/eval_jaxpr/dot_general | solution.py:31
  100.2 4.3 %fusion.47 = f32[24,192]{1,0:T(8,128)S(1)} fusion(f32[2048]{0:T(1024)S(1)} %get-tuple-element.335, s32[2048]{0:T(1024)S(1)} %get-tuple-element.336, f32[2048]{0:T(1024)S(1)} %get-tuple-element.337, s32[2048]{0:T(1024)S(1)} %get-tuple-element.338, f32[2048]{0:T(1024)S(1)} %dynamic_slice.57, f32[2048]{0:T(1024)S(1)} %get-tuple-element.339, ...), kind=kOutput, calls=%fused_computation.12.clone.1 | convolution fusion | flops 115516416 | bytes 110593 | tf_op jit(solution)/shard_map/while/body/eval_jaxpr/dot_general | solution.py:31
  104.6 4.3 %fusion.47 = f32[24,192]{1,0:T(8,128)S(1)} fusion(f32[2048]{0:T(1024)S(1)} %get-tuple-element.335, s32[2048]{0:T(1024)S(1)} %get-tuple-element.336, f32[2048]{0:T(1024)S(1)} %get-tuple-element.337, s32[2048]{0:T(1024)S(1)} %get-tuple-element.338, f32[2048]{0:T(1024)S(1)} %dynamic_slice.57, f32[2048]{0:T(1024)S(1)} %get-tuple-element.339, ...), kind=kOutput, calls=%fused_computation.12.clone.1 | convolution fusion | flops 115516416 | bytes 110593 | tf_op jit(solution)/shard_map/while/body/eval_jaxpr/dot_general | solution.py:31
  109.0 4.3 %fusion.47 = f32[24,192]{1,0:T(8,128)S(1)} fusion(f32[2048]{0:T(1024)S(1)} %get-tuple-element.335, s32[2048]{0:T(1024)S(1)} %get-tuple-element.336, f32[2048]{0:T(1024)S(1)} %get-tuple-element.337, s32[2048]{0:T(1024)S(1)} %get-tuple-element.338, f32[2048]{0:T(1024)S(1)} %dynamic_slice.57, f32[2048]{0:T(1024)S(1)} %get-tuple-element.339, ...), kind=kOutput, calls=%fused_computation.12.clone.1 | convolution fusion | flops 115516416 | bytes 110593 | tf_op jit(solution)/shard_map/while/body/eval_jaxpr/dot_general | solution.py:31
  113.4 4.3 %fusion.47 = f32[24,192]{1,0:T(8,128)S(1)} fusion(f32[2048]{0:T(1024)S(1)} %get-tuple-element.335, s32[2048]{0:T(1024)S(1)} %get-tuple-element.336, f32[2048]{0:T(1024)S(1)} %get-tuple-element.337, s32[2048]{0:T(1024)S(1)} %get-tuple-element.338, f32[2048]{0:T(1024)S(1)} %dynamic_slice.57, f32[2048]{0:T(1024)S(1)} %get-tuple-element.339, ...), kind=kOutput, calls=%fused_computation.12.clone.1 | convolution fusion | flops 115516416 | bytes 110593 | tf_op jit(solution)/shard_map/while/body/eval_jaxpr/dot_general | solution.py:31
  117.9 4.3 %fusion.47 = f32[24,192]{1,0:T(8,128)S(1)} fusion(f32[2048]{0:T(1024)S(1)} %get-tuple-element.335, s32[2048]{0:T(1024)S(1)} %get-tuple-element.336, f32[2048]{0:T(1024)S(1)} %get-tuple-element.337, s32[2048]{0:T(1024)S(1)} %get-tuple-element.338, f32[2048]{0:T(1024)S(1)} %dynamic_slice.57, f32[2048]{0:T(1024)S(1)} %get-tuple-element.339, ...), kind=kOutput, calls=%fused_computation.12.clone.1 | convolution fusion | flops 115516416 | bytes 110593 | tf_op jit(solution)/shard_map/while/body/eval_jaxpr/dot_general | solution.py:31
  122.3 4.3 %fusion.47 = f32[24,192]{1,0:T(8,128)S(1)} fusion(f32[2048]{0:T(1024)S(1)} %get-tuple-element.335, s32[2048]{0:T(1024)S(1)} %get-tuple-element.336, f32[2048]{0:T(1024)S(1)} %get-tuple-element.337, s32[2048]{0:T(1024)S(1)} %get-tuple-element.338, f32[2048]{0:T(1024)S(1)} %dynamic_slice.57, f32[2048]{0:T(1024)S(1)} %get-tuple-element.339, ...), kind=kOutput, calls=%fused_computation.12.clone.1 | convolution fusion | flops 115516416 | bytes 110593 | tf_op jit(solution)/shard_map/while/body/eval_jaxpr/dot_general | solution.py:31
  126.7 4.3 %fusion.47 = f32[24,192]{1,0:T(8,128)S(1)} fusion(f32[2048]{0:T(1024)S(1)} %get-tuple-element.335, s32[2048]{0:T(1024)S(1)} %get-tuple-element.336, f32[2048]{0:T(1024)S(1)} %get-tuple-element.337, s32[2048]{0:T(1024)S(1)} %get-tuple-element.338, f32[2048]{0:T(1024)S(1)} %dynamic_slice.57, f32[2048]{0:T(1024)S(1)} %get-tuple-element.339, ...), kind=kOutput, calls=%fused_computation.12.clone.1 | convolution fusion | flops 115516416 | bytes 110593 | tf_op jit(solution)/shard_map/while/body/eval_jaxpr/dot_general | solution.py:31
  131.0 10.3 %psum.7 = f32[24,192]{1,0:T(8,128)S(1)} all-reduce(f32[24,192]{1,0:T(8,128)S(1)} %get-tuple-element.212), channel_id=1, replica_groups=mesh['mem'=4,'lat'=16,'lon'=4] {'mem'}, use_global_device_ids=true, to_apply=%region_7.8 | all-reduce | flops 4608 | bytes 36864 | tf_op jit(solution)/shard_map/psum | solution.py:81
  141.5 26.8 %all_to_all.83 = bf16[16,4,24,192]{3,2,1,0:T(8,128)(2,1)S(1)} all-to-all(bf16[16,4,24,192]{3,2,1,0:T(8,128)(2,1)S(1)} %multiply_convert_fusion), channel_id=1, replica_groups=mesh['mem'=4,'lat'=16,'lon'=4] {'lat'}, dimensions={0} | all-to-all | bytes 1179648 | tf_op jit(solution)/shard_map/all_to_all | solution.py:86
  169.0 0.9 copy.33
  169.9 26.8 %all_to_all.84 = bf16[1,4,384,192]{3,1,0,2:T(4,128)(2,1)S(1)} all-to-all(bf16[1,4,384,192]{3,1,0,2:T(4,128)(2,1)S(1)} %copy.33), channel_id=1, replica_groups=mesh['mem'=4,'lat'=16,'lon'=4] {'lat'}, dimensions={2} | all-to-all | bytes 1179648 | tf_op jit(solution)/shard_map/all_to_all | solution.py:89
  196.9 12.0 %all_to_all.85 = bf16[16,4,24,192]{3,2,1,0:T(8,128)(2,1)S(1)} all-to-all(bf16[16,4,24,192]{3,2,1,0:T(8,128)(2,1)S(1)} %copy.35), channel_id=1, replica_groups=mesh['mem'=4,'lat'=16,'lon'=4] {'lon'}, dimensions={0} | all-to-all | bytes 1179648 | tf_op jit(solution)/shard_map/all_to_all | solution.py:92
  208.9 0.6 copy.45
  209.5 0.7 all_to_all.72
  210.2 0.6 convolution_convert_fusion
  210.9 4.1 %copy.37 = bf16[4,4,24,768]{2,1,0,3:T(4,128)(2,1)} copy(bf16[4,4,24,768]{3,2,1,0:T(8,128)(2,1)S(1)} %convolution_convert_fusion) | data formatting | bytes 1179648 | tf_op jit(solution)/shard_map/convert_element_type | solution.py:95
  215.0 5.3 %reshape.77 = bf16[4,2,36864]{2,1,0:T(2,128)(2,1)S(1)} reshape(bf16[768,4,4,24]{3,2,1,0:T(4,128)(2,1)} %bitcast.67) | data formatting | bytes 1179648
  220.2 10.8 %all_to_all.86 = bf16[4,2,36864]{2,1,0:T(2,128)(2,1)S(1)} all-to-all(bf16[4,2,36864]{2,1,0:T(2,128)(2,1)S(1)} %reshape.77), channel_id=1, replica_groups=mesh['mem'=4,'lat'=16,'lon'=4] {'lon'}, dimensions={0} | all-to-all | bytes 1179648 | tf_op jit(solution)/shard_map/all_to_all | solution.py:96
  231.1 5.3 %reshape.78 = bf16[768,4,4,24]{3,2,1,0:T(4,128)(2,1)} reshape(bf16[4,2,36864]{2,1,0:T(2,128)(2,1)S(1)} %all_to_all.86) | data formatting | bytes 1179648
  236.4 6.3 %copy.38 = bf16[4,4,4,24,192]{4,3,2,1,0:T(8,128)(2,1)} copy(bf16[4,4,4,24,192]{3,2,1,4,0:T(4,128)(2,1)} %bitcast.68) | data formatting | bytes 1179648 | tf_op jit(solution)/shard_map/all_to_all | solution.py:96
  (51 shorter events, 2.9 us)
Async XLA Ops:
  0.0 210.2 %copy-start = (bf16[768,768]{1,0:T(8,128)(2,1)S(1)}, bf16[768,768]{1,0:T(8,128)(2,1)}, u32[]{:S(2)}) copy-start(bf16[768,768]{1,0:T(8,128)(2,1)} %param.15) | copy-start | bytes 3538948
  19.7 1.0 copy-start.3
  19.7 1.9 copy-start.4
  19.7 2.0 copy-start.5
  42.7 30.8 %all-to-all-start.1 = ((f32[64,3,256]{2,1,0:T(4,128)}), f32[64,3,256]{2,1,0:T(4,128)S(1)}, u32[]{:S(2)}, u32[]{:S(2)}) async-start(f32[64,3,256]{2,1,0:T(4,128)} %bitcast.10), calls=%async_computation.1 | async-start | bytes 524288 | tf_op jit(solution)/shard_map/all_to_all | solution.py:59
  73.5 22.2 %all-to-all-start = ((s32[64,1,256]{2,1,0:T(1,128)}), s32[64,1,256]{2,1,0:T(1,128)S(1)}, u32[]{:S(2)}, u32[]{:S(2)}) async-start(s32[64,1,256]{2,1,0:T(1,128)} %bitcast.4), calls=%async_computation | async-start | bytes 131072 | tf_op jit(solution)/shard_map/all_to_all | solution.py:60
  95.7 45.6 %copy-start.1 = (bf16[16,4,24,192]{3,2,1,0:T(8,128)(2,1)S(1)}, bf16[16,4,24,192]{3,2,1,0:T(8,128)(2,1)}, u32[]{:S(2)}) copy-start(bf16[16,4,24,192]{3,2,1,0:T(8,128)(2,1)} %param.9) | copy-start | bytes 1769476
  141.3 27.1 %copy-start.2 = (bf16[384,384]{1,0:T(8,128)(2,1)S(1)}, bf16[384,384]{1,0:T(8,128)(2,1)}, u32[]{:S(2)}) copy-start(bf16[384,384]{1,0:T(8,128)(2,1)} %param.14) | copy-start | bytes 884740
where the time goes:
time: 247 us; the launch traced here: 243 us
  blocking collectives  86.7 us (35%)
  local copies, waits for them, and re-layouts  61.6 us (25%)
  matrix products  35.8 us (14%)
  starting transfers between devices  27.3 us (11%)
  other arithmetic  21.3 us (9%)
  waiting for transfers between devices  9.28 us (4%)
    dot_general x8, matrix products, add_block(): jnp.dot(row_table.T, col_table, precision=lax.Precision.HIGHEST, preferre...  34.6 us
    all_to_all x1, blocking collectives, shards(): lax.all_to_all(mixed, 'lat', split_axis=2, concat_axis=0, tiled=True)  26.8 us
    all_to_all x1, blocking collectives, shards(): lax.all_to_all(weighted, 'lat', split_axis=0, concat_axis=2, tiled=True)  26.8 us
    another operation x3, other arithmetic  19 us
    scatter x1, local copies, waits for them, and re-layouts, deliver(): integers = jnp.zeros((tile_count * capacity,), jnp.int32).at[slot_index]....  16.3 us
    all_to_all x1, starting transfers between devices, deliver(): lax.all_to_all(floats, ('lat', 'lon'), split_axis=0, concat_axis=0, tiled...  14.5 us
    scatter x1, local copies, waits for them, and re-layouts, deliver(): jnp.zeros((tile_count * capacity, 3), jnp.float32).at[slot_index]  14.3 us
    all_to_all x1, starting transfers between devices, deliver(): lax.all_to_all(integers, ('lat', 'lon'), split_axis=0, concat_axis=0, til...  12.8 us
  transfers between devices with their start and end apart: 2, of which 1 were waited for; matrix products, arithmetic and copies ran while one was open for 7% of the time, Pallas kernels for 0%

commit v1 on v0

v1 whole, which is shorter than its diff:
```python
import functools

import jax
import jax.numpy as jnp
from jax import lax
from jax.experimental import pallas as pl
from jax.experimental.pallas import tpu as pltpu
from jax.sharding import PartitionSpec as P

MESH = pl.DeviceIdType.MESH
F32 = jnp.float32
BF16 = jnp.bfloat16

LEVELS, ROWS, COLS = 4, 24, 192
LAT, LON, OBS = 384, 768, 4096
HALF = LON // 2
PLANE, DEPTH, GROUP = 16, 8, 64
CHUNK = 2048
PACKED = 40


def tent_table(index, low, high, count):
    width = index.shape[1]
    low, high = low.astype(BF16), high.astype(BF16)
    rows = lax.broadcasted_iota(jnp.int32, (128, width), 0).astype(F32).astype(BF16)
    parts = []
    for base in range(0, count, 128):
        at = (index - base).astype(BF16)
        after = (index - (base - 1)).astype(BF16)
        parts.append(jnp.where(rows == at, low, jnp.where(rows == after, high, BF16(0))))
    return jnp.concatenate(parts, axis=0)


def kernel(
    anom, innov, frac, cell, owner, lat_k, lon_k, out,
    v_innov, v_frac, v_cell, v_owner, v_latk, v_lonk,
    obs, row_table, col_table, total,
    psend, precv, zsend, zrecv, forcing,
    xrecv, fsend, frecv, lat_t, weighted, gsend, grecv, out_v,
    load_sem, own_sem, out_sem,
    obs_sem, x_sem, p_sem, z_sem, f_sem, ag_send, ag_recv, core_sem, g_send, g_recv,
):
    mem, lat, lon = lax.axis_index("mem"), lax.axis_index("lat"), lax.axis_index("lon")
    core, y_lo = lax.rem(mem, 2), mem // 2
    z, y_hi = lax.rem(lat, 8), lat // 8
    q = (y_hi * 2 + y_lo) * 4 + lon
    e = y_hi * 4 + lon
    me = lat * 4 + lon
    mate = {"mem": mem + 1 - 2 * core}

    def plane_peer(p):
        y = p // 4
        return {"mem": lax.rem(y, 2) * 2 + core, "lat": (y // 2) * 8 + z, "lon": lax.rem(p, 4)}

    def z_peer(to):
        return {"lat": y_hi * 8 + to}

    def remote(src, dst, send, recv, to):
        return pltpu.make_async_remote_copy(
            src_ref=src, dst_ref=dst, send_sem=send, recv_sem=recv, device_id=to, device_id_type=MESH
        )

    loads = [
        pltpu.make_async_copy(src, dst, load_sem.at[i])
        for i, (src, dst) in enumerate(
            ((innov, v_innov), (frac, v_frac), (cell, v_cell), (owner, v_owner), (lat_k, v_latk), (lon_k, v_lonk))
        )
    ]
    for load in loads:
        load.start()
    own_x = pltpu.make_async_copy(anom.at[pl.ds(y_hi * 8, 8), lon], xrecv.at[e], own_sem.at[0])
    own_x.start()

    barrier = pltpu.get_barrier_semaphore()

    def greet_plane(s, carry):
        pl.semaphore_signal(barrier, inc=1, device_id=plane_peer(lax.rem(q + s, PLANE)), device_id_type=MESH)
        return carry

    def greet_z(s, carry):
        pl.semaphore_signal(barrier, inc=1, device_id=z_peer(lax.rem(z + s, DEPTH)), device_id_type=MESH)
        return carry

    lax.fori_loop(1, PLANE, greet_plane, 0)
    lax.fori_loop(1, DEPTH, greet_z, 0)
    pl.semaphore_signal(barrier, inc=1, device_id=mate, device_id_type=MESH)

    for load in loads[:4]:
        load.wait()
    cells = v_cell[...]
    cell_row = ((cells.astype(F32) + 0.5) * (1.0 / COLS)).astype(jnp.int32)
    cell_col = cells - cell_row * COLS
    tile = v_owner[...]
    value, a, b = v_innov[...], v_frac[0:1, :], v_frac[1:2, :]
    obs[0, 0:1, :] = ((tile >> 2) * ROWS + cell_row).astype(F32)
    obs[0, 1:2, :] = ((tile & 3) * COLS + cell_col).astype(F32)
    obs[0, 2:3, :] = value * (1.0 - a)
    obs[0, 3:4, :] = value * a
    obs[0, 4:5, :] = 1.0 - b
    obs[0, 5:6, :] = b
    obs[0, 6:8, :] = jnp.zeros((2, OBS), F32)

    first_col = (core * HALF).astype(F32)

    def spread(slot, start, first):
        at = pl.ds(start, CHUNK)
        row_table[...] = tent_table(obs[slot, 0:1, at], obs[slot, 2:3, at], obs[slot, 3:4, at], LAT)
        col_table[...] = tent_table(obs[slot, 1:2, at] - first_col, obs[slot, 4:5, at], obs[slot, 5:6, at], HALF)
        product = lax.dot_general(
            row_table[...], col_table[...], (((1,), (1,)), ((), ())), preferred_element_type=F32
        )
        if first:
            total[...] = product
        else:
            total[...] += product

    spread(0, 0, True)

    pl.semaphore_wait(barrier, PLANE - 1 + DEPTH - 1 + 1)
    obs_copy = remote(obs.at[0], obs.at[1], obs_sem.at[0], obs_sem.at[1], mate)
    obs_copy.start()

    def send_x(s, carry):
        to = lax.rem(e + s, 8)
        to_y, to_x = to // 4, lax.rem(to, 4)
        remote(
            anom.at[pl.ds(to_y * 8, 8), to_x], xrecv.at[e], x_sem.at[0], x_sem.at[1],
            {"lat": to_y * 8 + z, "lon": to_x},
        ).start()
        return carry

    lax.fori_loop(1, 8, send_x, 0)

    spread(0, CHUNK, False)
    obs_copy.wait_recv()
    spread(1, 0, False)
    spread(1, CHUNK, False)

    for p in range(PLANE):
        psend[p] = total[ROWS * p : ROWS * (p + 1), :].astype(BF16)

    def send_p(s, carry):
        to = lax.rem(q + s, PLANE)
        remote(psend.at[to], precv.at[q], p_sem.at[0], p_sem.at[1], plane_peer(to)).start()
        return carry

    lax.fori_loop(1, PLANE, send_p, 0)

    loads[4].wait()
    lat_t[...] = v_latk[...].astype(F32).T.astype(BF16)

    remote(
        psend.at[pl.ds(0, PLANE - 1)], precv.at[pl.ds(0, PLANE - 1)], p_sem.at[0], p_sem.at[1], mate
    ).wait_recv()
    band = total[pl.ds(pl.multiple_of(q * ROWS, 8), ROWS), :]
    for s in range(1, PLANE):
        band = band + precv[lax.rem(q + s, PLANE)].astype(F32)

    zsend[...] = band.astype(BF16)

    def send_z(s, carry):
        to = lax.rem(z + s, DEPTH)
        remote(zsend, zrecv.at[z], z_sem.at[0], z_sem.at[1], z_peer(to)).start()
        return carry

    lax.fori_loop(1, DEPTH, send_z, 0)

    remote(
        xrecv.at[pl.ds(0, 7)], xrecv.at[pl.ds(0, 7)], x_sem.at[0], x_sem.at[1], mate
    ).wait_recv()
    own_x.wait()
    for to in range(DEPTH):
        for y in range(2):
            fsend[to, ROWS * y : ROWS * (y + 1), :] = jnp.concatenate(
                [xrecv[y * 4 + x, to].astype(F32) for x in range(4)], axis=1
            ).astype(BF16)

    def send_f(s, carry):
        to = lax.rem(z + s, DEPTH)
        remote(fsend.at[to], frecv.at[z], f_sem.at[0], f_sem.at[1], z_peer(to)).start()
        return carry

    lax.fori_loop(1, DEPTH, send_f, 0)
    own_f = pltpu.make_async_copy(fsend.at[z], frecv.at[z], own_sem.at[1])
    own_f.start()

    remote(
        zrecv.at[pl.ds(0, DEPTH - 1)], zrecv.at[pl.ds(0, DEPTH - 1)], z_sem.at[0], z_sem.at[1], mate
    ).wait_recv()
    for s in range(1, DEPTH):
        band = band + zrecv[lax.rem(z + s, DEPTH)].astype(F32)
    forcing[core, q] = band.astype(BF16)

    def send_ag(s, carry):
        to = lax.rem(q + s, PLANE)
        remote(forcing.at[core, q], forcing.at[core, q], ag_send, ag_recv.at[q], plane_peer(to)).start()
        return carry

    lax.fori_loop(1, PLANE, send_ag, 0)

    def to_mate(p):
        return remote(forcing.at[core, p], forcing.at[core, p], core_sem.at[0], core_sem.at[1], mate)

    to_mate(q).start()

    def pass_on(s, carry):
        p = lax.rem(q + PLANE - s, PLANE)
        remote(forcing.at[core, p], forcing.at[core, p], ag_send, ag_recv.at[p], mate).wait_recv()
        to_mate(p).start()
        return carry

    lax.fori_loop(1, PLANE, pass_on, 0)

    remote(
        frecv.at[pl.ds(0, DEPTH - 1)], frecv.at[pl.ds(0, DEPTH - 1)], f_sem.at[0], f_sem.at[1], mate
    ).wait_recv()
    own_f.wait()
    loads[5].wait()
    remote(forcing.at[1 - core], forcing.at[1 - core], core_sem.at[0], core_sem.at[1], mate).wait_recv()

    for t in range(DEPTH):
        pair = []
        for band_at in (2 * t, 2 * t + 1):
            y, at = band_at // 8, band_at % 8
            field = frecv[at, ROWS * y : ROWS * (y + 1), :].astype(F32)
            factor = jnp.concatenate([forcing[0, band_at], forcing[1, band_at]], axis=1).astype(F32)
            pair.append(field * factor)
        weighted[2 * ROWS * t : 2 * ROWS * (t + 1), :] = jnp.concatenate(pair, axis=0).astype(BF16)

    low_lanes = lax.broadcasted_iota(jnp.int32, (8, 128), 1) < 64
    low_wide = lax.broadcasted_iota(jnp.int32, (ROWS, 128), 1) < 64

    for h in range(2):
        mixed = jnp.dot(lat_t[LAT // 2 * h : LAT // 2 * (h + 1), :], weighted[...], preferred_element_type=F32)
        grad = jnp.dot(mixed.astype(BF16), v_lonk[...], preferred_element_type=F32)
        for i in range(8):
            for pair_at in range(2):
                t0, t1, t2 = (
                    grad[ROWS * i : ROWS * (i + 1), 384 * pair_at + 128 * j : 384 * pair_at + 128 * (j + 1)]
                    for j in range(3)
                )
                r1, r2 = pltpu.roll(t1, 64, 1), pltpu.roll(t2, 64, 1)
                for odd, (main, low, high) in enumerate(
                    ((t0, t1, r1), (jnp.where(low_wide, r1, r2), r2, t2))
                ):
                    tail = jnp.where(low_lanes, low[0:8], high[8:16])
                    gsend[(8 * h + i) * 4 + 2 * pair_at + odd] = jnp.concatenate(
                        [main, tail, low[16:24]], axis=0
                    ).astype(BF16)

        def send_g(s, carry):
            to_lat = 8 * h + lax.rem(z + s // 4, 8)
            to_lon = lax.rem(lon + s, 4)
            to = to_lat * 4 + to_lon

            @pl.when(to != me)
            def _():
                remote(
                    gsend.at[to], grecv.at[me], g_send, g_recv.at[lat], {"lat": to_lat, "lon": to_lon}
                ).start()

            return carry

        lax.fori_loop(0, 32, send_g, 0)

    own_g = pltpu.make_async_copy(gsend.at[me], grecv.at[me], own_sem.at[2])
    own_g.start()
    own_g.wait()

    def take(s, carry):
        at = lax.rem(lat + s, 16)

        @pl.when(s == 0)
        def _():
            remote(grecv.at[pl.ds(0, 3)], grecv.at[pl.ds(0, 3)], g_send, g_recv.at[at], mate).wait_recv()

        @pl.when(s != 0)
        def _():
            remote(grecv.at[pl.ds(0, 4)], grecv.at[pl.ds(0, 4)], g_send, g_recv.at[at], mate).wait_recv()

        for k in range(LEVELS):
            block = grecv[at * 4 + k].astype(F32)
            tail = block[24:32]
            out_v[at, k, :, 0:128] = block[0:24].astype(BF16)
            out_v[at, k, :, 128:192] = jnp.concatenate(
                [tail, pltpu.roll(tail, 64, 1), block[32:40]], axis=0
            )[:, 0:64].astype(BF16)
        pltpu.make_async_copy(out_v.at[at], out.at[at], out_sem).start()
        return carry

    lax.fori_loop(0, 16, take, 0)
    pltpu.make_async_copy(out_v, out, out_sem).wait()

    obs_copy.wait_send()
    remote(xrecv.at[pl.ds(0, 7)], xrecv.at[pl.ds(0, 7)], x_sem.at[0], x_sem.at[1], mate).wait_send()
    remote(psend.at[pl.ds(0, 15)], psend.at[pl.ds(0, 15)], p_sem.at[0], p_sem.at[1], mate).wait_send()
    remote(zrecv.at[pl.ds(0, 7)], zrecv.at[pl.ds(0, 7)], z_sem.at[0], z_sem.at[1], mate).wait_send()
    remote(fsend.at[pl.ds(0, 7)], fsend.at[pl.ds(0, 7)], f_sem.at[0], f_sem.at[1], mate).wait_send()
    remote(psend.at[pl.ds(0, 15)], psend.at[pl.ds(0, 15)], ag_send, p_sem.at[1], mate).wait_send()
    remote(forcing.at[0], forcing.at[0], core_sem.at[0], core_sem.at[1], mate).wait_send()
    remote(gsend.at[pl.ds(0, 63)], gsend.at[pl.ds(0, 63)], g_send, p_sem.at[1], mate).wait_send()


def shards(anomalies, innovation, corner_frac, corner_cell, cell_owner, latitude_kernel, longitude_kernel):
    dma = pltpu.SemaphoreType.DMA
    return pl.pallas_call(
        kernel,
        out_shape=jax.ShapeDtypeStruct(anomalies.shape, BF16),
        in_specs=[pl.BlockSpec(memory_space=pl.ANY)] * 7,
        out_specs=pl.BlockSpec(memory_space=pl.ANY),
        scratch_shapes=[
            pltpu.VMEM((1, OBS), F32),
            pltpu.VMEM((2, OBS), F32),
            pltpu.VMEM((1, OBS), jnp.int32),
            pltpu.VMEM((1, OBS), jnp.int32),
            pltpu.VMEM((LAT, LAT), BF16),
            pltpu.VMEM((LON, LON), BF16),
            pltpu.VMEM((2, 8, OBS), F32),
            pltpu.VMEM((LAT, CHUNK), BF16),
            pltpu.VMEM((HALF, CHUNK), BF16),
            pltpu.VMEM((LAT, HALF), F32),
            pltpu.VMEM((PLANE, ROWS, HALF), BF16),
            pltpu.VMEM((PLANE, ROWS, HALF), BF16),
            pltpu.VMEM((ROWS, HALF), BF16),
            pltpu.VMEM((DEPTH, ROWS, HALF), BF16),
            pltpu.VMEM((2, PLANE, ROWS, HALF), BF16),
            pltpu.VMEM((8, 8, ROWS, COLS), BF16),
            pltpu.VMEM((DEPTH, 2 * ROWS, LON), BF16),
            pltpu.VMEM((DEPTH, 2 * ROWS, LON), BF16),
            pltpu.VMEM((LAT, LAT), BF16),
            pltpu.VMEM((LAT, LON), BF16),
            pltpu.VMEM((GROUP, PACKED, 128), BF16),
            pltpu.VMEM((GROUP, PACKED, 128), BF16),
            pltpu.VMEM((16, LEVELS, ROWS, COLS), BF16),
            dma((6,)),
            dma((3,)),
            dma,
            dma((2,)),
            dma((2,)),
            dma((2,)),
            dma((2,)),
            dma((2,)),
            dma,
            dma((PLANE,)),
            dma((2,)),
            dma,
            dma((16,)),
        ],
        compiler_params=pltpu.CompilerParams(
            collective_id=0, has_side_effects=True, vmem_limit_bytes=40 * 2**20
        ),
    )(
        anomalies,
        innovation.reshape(1, OBS),
        corner_frac,
        corner_cell.reshape(1, OBS),
        cell_owner.reshape(1, OBS),
        latitude_kernel,
        longitude_kernel,
    )


def solution(mesh):
    placed = (
        P("mem", None, "lat", "lon"),
        P(("mem", "lat", "lon")),
        P(None, ("mem", "lat", "lon")),
        P(("mem", "lat", "lon")),
        P(("mem", "lat", "lon")),
        P(),
        P(),
    )
    return jax.shard_map(
        shards, mesh=mesh, in_specs=placed, out_specs=P("mem", None, "lat", "lon"), check_vma=False
    )
```

time: 247 us -> 70.3 us (0.28); the launches traced: 243 us -> 69.5 us
  blocking collectives: 86.7 us -> 0 us
  Pallas kernels: 0 us -> 62.3 us
  local copies, waits for them, and re-layouts: 61.6 us -> 7.15 us
  matrix products: 35.8 us -> 0 us
  starting transfers between devices: 27.3 us -> 0 us
  other arithmetic: 21.3 us -> 0 us
  waiting for transfers between devices: 9.28 us -> 0 us
    all_to_all x4 -> x0, blocking collectives: 76.5 us -> none  [the longest x1 26.8 us: shards(): lax.all_to_all(mixed, 'lat', split_axis=2, concat_axis=0, tiled=True)]
    pallas_call x0 -> x1, Pallas kernels: none -> 62.3 us  [shards(): pl.pallas_call(kernel, out_shape=jax.ShapeDtypeStruct(anomalies.shape, BF...]
    dot_general x10 -> x0, matrix products: 35.8 us -> none  [the longest x8 34.6 us: add_block(): jnp.dot(row_table.T, col_table, precision=lax.Precision.HIGHEST, preferre...]
    scatter x2 -> x0, local copies, waits for them, and re-layouts: 30.6 us -> none  [the longest x1 16.3 us: deliver(): integers = jnp.zeros((tile_count * capacity,), jnp.int32).at[slot_index]....]
    all_to_all x2 -> x0, starting transfers between devices: 27.3 us -> none  [the longest x1 14.5 us: deliver(): lax.all_to_all(floats, ('lat', 'lon'), split_axis=0, concat_axis=0, tiled...]
    another operation x4 -> x0, other arithmetic: 19 us -> none
    psum x1 -> x0, blocking collectives: 10.3 us -> none  [shards(): forcing = lax.psum(partial_grid, 'mem')]
    all_to_all x2 -> x0, waiting for transfers between devices: 9.28 us -> none  [the longest x1 9.27 us: deliver(): lax.all_to_all(integers, ('lat', 'lon'), split_axis=0, concat_axis=0, til...]
  transfers between devices with their start and end apart: 2 -> 0, of which waited for: 1 -> 0; matrix products, arithmetic and copies ran while one was open for 7% -> 0% of each run, Pallas kernels for 0% -> 0%
where the time goes in v1:
time: 70.3 us; the launch traced here: 69.5 us
  Pallas kernels  62.3 us (89%)
  local copies, waits for them, and re-layouts  7.15 us (10%)
    pallas_call x1, Pallas kernels, shards(): pl.pallas_call(kernel, out_shape=jax.ShapeDtypeStruct(anomalies.shape, BF...  62.3 us
    unnamed x15, local copies, waits for them, and re-layouts  7.15 us

profile of v1, /device:TPU:16, one launch (start us, length us, event | category | flops | bytes accessed | tf_op | source)
XLA Modules:
  0.0 69.5 jit_solution(13495400807702675864)
XLA Ops:
  0.0 0.0 copy-start
  0.0 1.3 %copy-done = bf16[768,768]{1,0:T(8,128)(2,1)S(1)} copy-done((bf16[768,768]{1,0:T(8,128)(2,1)S(1)}, bf16[768,768]{1,0:T(8,128)(2,1)}, u32[]{:S(2)}) %copy-start) | copy-done | bytes 1179672
  1.3 0.0 copy-start.1
  1.3 1.1 %copy-done.1 = bf16[16,4,24,192]{3,2,1,0:T(8,128)(2,1)S(1)} copy-done((bf16[16,4,24,192]{3,2,1,0:T(8,128)(2,1)S(1)}, bf16[16,4,24,192]{3,2,1,0:T(8,128)(2,1)}, u32[]{:S(2)}) %copy-start.1) | copy-done | bytes 589848
  2.4 0.0 copy-start.2
  2.4 1.0 %copy-done.2 = bf16[384,384]{1,0:T(8,128)(2,1)S(1)} copy-done((bf16[384,384]{1,0:T(8,128)(2,1)S(1)}, bf16[384,384]{1,0:T(8,128)(2,1)}, u32[]{:S(2)}) %copy-start.2) | copy-done | bytes 294936
  3.4 0.0 copy-start.3
  3.4 0.8 %copy-done.3 = f32[2,4096]{1,0:T(2,128)S(1)} copy-done((f32[2,4096]{1,0:T(2,128)S(1)}, f32[2,4096]{1,0:T(2,128)}, u32[]{:S(2)}) %copy-start.3) | copy-done | bytes 32792
  4.1 0.0 copy-start.4
  4.1 0.7 %copy-done.4 = f32[4096]{0:T(1024)S(1)} copy-done((f32[4096]{0:T(1024)S(1)}, f32[4096]{0:T(1024)}, u32[]{:S(2)}) %copy-start.4) | copy-done | bytes 16408
  4.8 0.0 copy-start.5
  4.8 0.7 %copy-done.5 = s32[4096]{0:T(1024)S(1)} copy-done((s32[4096]{0:T(1024)S(1)}, s32[4096]{0:T(1024)}, u32[]{:S(2)}) %copy-start.5) | copy-done | bytes 16408
  5.6 0.0 copy-start.6
  5.6 0.7 %copy-done.6 = s32[4096]{0:T(1024)S(1)} copy-done((s32[4096]{0:T(1024)S(1)}, s32[4096]{0:T(1024)}, u32[]{:S(2)}) %copy-start.6) | copy-done | bytes 16408
  6.3 62.3 %shard_map.73 = bf16[16,4,24,192]{3,2,1,0:T(8,128)(2,1)S(1)} custom-call(bf16[16,4,24,192]{3,2,1,0:T(8,128)(2,1)S(1)} %copy-done.1, f32[1,4096]{1,0:T(1,128)S(1)} %bitcast.3, f32[2,4096]{1,0:T(2,128)S(1)} %copy-done.3, s32[1,4096]{1,0:T(1,128)S(1)} %bitcast.4, s32[1,4096]{1,0:T(1,128)S(1)} %bitcast.5, bf16[384,384]{1,0:T(8,128)(2,1)S(1)} %copy-done.2, ...), custom_call_target="tpu_custom_call" | custom-call | tf_op jit(solution)/shard_map/pallas_call | solution.py:306
  68.6 0.9 %copy.9 = bf16[16,4,24,192]{3,2,1,0:T(8,128)(2,1)} copy(bf16[16,4,24,192]{3,2,1,0:T(8,128)(2,1)S(1)} %shard_map.73) | data formatting | bytes 1179648
Async XLA Ops:
  0.0 1.3 %copy-start = (bf16[768,768]{1,0:T(8,128)(2,1)S(1)}, bf16[768,768]{1,0:T(8,128)(2,1)}, u32[]{:S(2)}) copy-start(bf16[768,768]{1,0:T(8,128)(2,1)} %lon_k.1) | copy-start | bytes 3538948
  1.3 1.1 %copy-start.1 = (bf16[16,4,24,192]{3,2,1,0:T(8,128)(2,1)S(1)}, bf16[16,4,24,192]{3,2,1,0:T(8,128)(2,1)}, u32[]{:S(2)}) copy-start(bf16[16,4,24,192]{3,2,1,0:T(8,128)(2,1)} %anom.1) | copy-start | bytes 1769476
  2.4 1.0 %copy-start.2 = (bf16[384,384]{1,0:T(8,128)(2,1)S(1)}, bf16[384,384]{1,0:T(8,128)(2,1)}, u32[]{:S(2)}) copy-start(bf16[384,384]{1,0:T(8,128)(2,1)} %lat_k.1) | copy-start | bytes 884740
  3.4 0.8 %copy-start.3 = (f32[2,4096]{1,0:T(2,128)S(1)}, f32[2,4096]{1,0:T(2,128)}, u32[]{:S(2)}) copy-start(f32[2,4096]{1,0:T(2,128)} %frac.1) | copy-start | bytes 98308
  4.1 0.7 %copy-start.4 = (f32[4096]{0:T(1024)S(1)}, f32[4096]{0:T(1024)}, u32[]{:S(2)}) copy-start(f32[4096]{0:T(1024)} %param.8) | copy-start | bytes 49156
  4.8 0.7 %copy-start.5 = (s32[4096]{0:T(1024)S(1)}, s32[4096]{0:T(1024)}, u32[]{:S(2)}) copy-start(s32[4096]{0:T(1024)} %param.10) | copy-start | bytes 49156
  5.6 0.7 %copy-start.6 = (s32[4096]{0:T(1024)S(1)}, s32[4096]{0:T(1024)}, u32[]{:S(2)}) copy-start(s32[4096]{0:T(1024)} %param.11) | copy-start | bytes 49156

commit v2 on v1

v2 whole, which is shorter than its diff:
```python
import functools

import jax
import jax.numpy as jnp
from jax import lax
from jax.experimental import pallas as pl
from jax.experimental.pallas import tpu as pltpu
from jax.sharding import PartitionSpec as P

MESH = pl.DeviceIdType.MESH
F32 = jnp.float32
BF16 = jnp.bfloat16

LEVELS, ROWS, COLS = 4, 24, 192
LAT, LON, OBS = 384, 768, 4096
HALF = LON // 2
PLANE, DEPTH, GROUP = 16, 8, 64
CHUNK = 2048
PACKED = 36


def tent_table(index, low, high, count):
    width = index.shape[1]
    low, high = low.astype(BF16), high.astype(BF16)
    rows = lax.broadcasted_iota(jnp.int32, (128, width), 0).astype(F32).astype(BF16)
    parts = []
    for base in range(0, count, 128):
        at = (index - base).astype(BF16)
        after = (index - (base - 1)).astype(BF16)
        parts.append(jnp.where(rows == at, low, jnp.where(rows == after, high, BF16(0))))
    return jnp.concatenate(parts, axis=0)


def unpack(packed):
    eight, four = packed[24:32], packed[32:36]
    tail = jnp.concatenate([eight[:, 0:64], eight[:, 64:128], four[:, 0:64], four[:, 64:128]], axis=0)
    return jnp.concatenate([packed[0:24], tail], axis=1)


def kernel(
    anom, innov, frac, cell, owner, lat_k, lon_k, out,
    v_innov, v_frac, v_cell, v_owner, v_latk, v_lonk,
    obs, row_table, col_table, total,
    psend, precv, zsend, zrecv, forcing,
    v_anom, fsend, frecv, field, lat_t, weighted, gsend, grecv,
    load_sem, own_sem,
    obs_sem, p_sem, z_sem, f_sem, x_sem, ag_sem, core_sem, g_send, g_recv,
):
    mem, lat, lon = lax.axis_index("mem"), lax.axis_index("lat"), lax.axis_index("lon")
    core, y_lo = lax.rem(mem, 2), mem // 2
    z, y_hi = lax.rem(lat, 8), lat // 8
    q = (y_hi * 2 + y_lo) * 4 + lon
    e = y_hi * 4 + lon
    me = lat * 4 + lon
    mate = {"mem": mem + 1 - 2 * core}

    def plane_peer(p):
        y = p // 4
        return {"mem": lax.rem(y, 2) * 2 + core, "lat": (y // 2) * 8 + z, "lon": lax.rem(p, 4)}

    def z_peer(to):
        return {"lat": y_hi * 8 + to}

    def remote(src, dst, send, recv, to):
        return pltpu.make_async_remote_copy(
            src_ref=src, dst_ref=dst, send_sem=send, recv_sem=recv, device_id=to, device_id_type=MESH
        )

    owed, sent = {}, []

    def expect(name, block, count, sems, start=0):
        some = block.at[pl.ds(0, count)]
        owed[name] = remote(some, some, sems.at[0], sems.at[1], mate).wait_recv
        sent.append(remote(some, some, sems.at[0], sems.at[1], mate).wait_send)

    loads = [
        pltpu.make_async_copy(src, dst, load_sem.at[i])
        for i, (src, dst) in enumerate(
            ((innov, v_innov), (frac, v_frac), (cell, v_cell), (owner, v_owner), (anom, v_anom), (lat_k, v_latk), (lon_k, v_lonk))
        )
    ]
    for i, load in enumerate(loads):
        load.start()
        owed[i] = load.wait

    barrier = pltpu.get_barrier_semaphore()

    def greet_plane(s, carry):
        pl.semaphore_signal(barrier, inc=1, device_id=plane_peer(lax.rem(q + s, PLANE)), device_id_type=MESH)
        return carry

    def greet_z(s, carry):
        pl.semaphore_signal(barrier, inc=1, device_id=z_peer(lax.rem(z + s, DEPTH)), device_id_type=MESH)
        return carry

    lax.fori_loop(1, PLANE, greet_plane, 0)
    lax.fori_loop(1, DEPTH, greet_z, 0)
    pl.semaphore_signal(barrier, inc=1, device_id=mate, device_id_type=MESH)

    for i in range(4):
        owed.pop(i)()
    cells = v_cell[...]
    cell_row = ((cells.astype(F32) + 0.5) * (1.0 / COLS)).astype(jnp.int32)
    cell_col = cells - cell_row * COLS
    tile = v_owner[...]
    value, a, b = v_innov[...], v_frac[0:1, :], v_frac[1:2, :]
    obs[0, 0:1, :] = ((tile >> 2) * ROWS + cell_row).astype(F32)
    obs[0, 1:2, :] = ((tile & 3) * COLS + cell_col).astype(F32)
    obs[0, 2:3, :] = value * (1.0 - a)
    obs[0, 3:4, :] = value * a
    obs[0, 4:5, :] = 1.0 - b
    obs[0, 5:6, :] = b
    obs[0, 6:8, :] = jnp.zeros((2, OBS), F32)

    first_col = (core * HALF).astype(F32)

    def tables(slot, start):
        at, use = pl.ds(start, CHUNK), (2 * slot + start // CHUNK) % 2
        row_table[use] = tent_table(obs[slot, 0:1, at], obs[slot, 2:3, at], obs[slot, 3:4, at], LAT)
        col_table[use] = tent_table(obs[slot, 1:2, at] - first_col, obs[slot, 4:5, at], obs[slot, 5:6, at], HALF)

    def spread(part):
        product = lax.dot_general(
            row_table[part % 2], col_table[part % 2], (((1,), (1,)), ((), ())), preferred_element_type=F32
        )
        if part == 0:
            total[...] = product
        else:
            total[...] += product

    tables(0, 0)

    owed.pop(4)()

    def pack(m, carry):
        for k in range(LEVELS):
            block = v_anom[m, k].astype(F32)
            tail = block[:, 128:192]
            fsend[lax.rem(m, 8), m // 8, k] = jnp.concatenate(
                [
                    block[:, 0:128],
                    jnp.concatenate([tail[0:8], tail[8:16]], axis=1),
                    jnp.concatenate([tail[16:20], tail[20:24]], axis=1),
                ],
                axis=0,
            ).astype(BF16)
        return carry

    lax.fori_loop(0, 16, pack, 0, unroll=2)

    pl.semaphore_wait(barrier, PLANE - 1 + DEPTH - 1 + 1)
    obs_copy = remote(obs.at[0], obs.at[1], obs_sem.at[0], obs_sem.at[1], mate)
    obs_copy.start()
    owed["obs"] = obs_copy.wait_recv
    sent.append(obs_copy.wait_send)

    offs = (4, 3, -3, 2, -2, 1, -1)

    def first_leg(leg, slots):
        for i in slots:
            to = lax.rem(z - offs[i - 1] + DEPTH, DEPTH)
            remote(fsend.at[to], frecv.at[i], f_sem.at[leg, 0], f_sem.at[leg, 1], z_peer(to)).start()
        expect("f%d" % leg, fsend, len(slots), f_sem.at[leg])

    first_leg(0, (1, 2, 3))
    own_f = pltpu.make_async_copy(fsend.at[z], frecv.at[0], own_sem.at[0])
    own_f.start()
    owed["own_f"] = own_f.wait

    spread(0)
    tables(0, CHUNK)
    owed.pop("obs")()
    spread(1)
    tables(1, 0)
    spread(2)
    tables(1, CHUNK)
    spread(3)

    for p in range(PLANE):
        psend[p] = total[ROWS * p : ROWS * (p + 1), :].astype(BF16)

    def send_p(s, carry):
        to = lax.rem(q + s, PLANE)
        remote(psend.at[to], precv.at[q], p_sem.at[0], p_sem.at[1], plane_peer(to)).start()
        return carry

    lax.fori_loop(1, PLANE, send_p, 0)
    expect("p", psend, PLANE - 1, p_sem)

    owed.pop(5)()
    lat_t[...] = v_latk[...].astype(F32).T.astype(BF16)

    owed.pop("p")()
    band = total[pl.ds(pl.multiple_of(q * ROWS, 8), ROWS), :]
    for s in range(1, PLANE):
        band = band + precv[lax.rem(q + s, PLANE)].astype(F32)

    zsend[...] = band.astype(BF16)

    def send_z(s, carry):
        to = lax.rem(z + s, DEPTH)
        remote(zsend, zrecv.at[z], z_sem.at[0], z_sem.at[1], z_peer(to)).start()
        return carry

    lax.fori_loop(1, DEPTH, send_z, 0)
    expect("z", zrecv, DEPTH - 1, z_sem)
    first_leg(1, (4, 5, 6, 7))

    def second_leg(half):
        slots = pl.ds(4 * half, 4)
        for i in range(1, 8):
            to = lax.rem(e + i, 8)
            to_y, to_x = to // 4, lax.rem(to, 4)
            remote(
                frecv.at[slots, to_y, to_x], field.at[e, slots], x_sem.at[half, 0], x_sem.at[half, 1],
                {"lat": to_y * 8 + z, "lon": to_x},
            ).start()
        some = field.at[pl.ds(0, 7), pl.ds(0, 4)]
        copy = remote(some, some, x_sem.at[half, 0], x_sem.at[half, 1], mate)
        owed["x%d" % half] = copy.wait_recv
        sent.append(copy.wait_send)

    owed.pop("f0")()
    owed.pop("own_f")()
    second_leg(0)

    owed.pop("z")()
    for s in range(1, DEPTH):
        band = band + zrecv[lax.rem(z + s, DEPTH)].astype(F32)
    forcing[core, q] = band.astype(BF16)

    def send_ag(s, carry):
        to = lax.rem(q + s, PLANE)
        remote(forcing.at[core, q], forcing.at[core, q], ag_sem.at[0], ag_sem.at[1], plane_peer(to)).start()
        return carry

    lax.fori_loop(1, PLANE, send_ag, 0)
    expect("ag", psend, PLANE - 1, ag_sem)
    owed.pop("f1")()
    second_leg(1)
    own_x = pltpu.make_async_copy(frecv.at[:, y_hi, lon], field.at[e], own_sem.at[1])
    own_x.start()
    owed["own_x"] = own_x.wait
    owed.pop("ag")()
    halves = remote(forcing.at[core], forcing.at[core], core_sem.at[0], core_sem.at[1], mate)
    halves.start()
    owed["half"] = halves.wait_recv
    sent.append(halves.wait_send)

    owed.pop("half")()
    owed.pop("x0")()
    owed.pop("x1")()
    owed.pop("own_x")()
    owed.pop(6)()

    for t in range(DEPTH):
        pair = []
        for band_at in (2 * t, 2 * t + 1):
            y, ahead = band_at // 8, lax.rem(band_at % 8 - z + DEPTH, DEPTH)
            slot = lax.rem(jnp.maximum(2 * ahead - 7, 8 - 2 * ahead), DEPTH)
            row = jnp.concatenate([unpack(field[y * 4 + x, slot].astype(F32)) for x in range(4)], axis=1)
            factor = jnp.concatenate([forcing[0, band_at], forcing[1, band_at]], axis=1).astype(F32)
            pair.append(row * factor)
        weighted[2 * ROWS * t : 2 * ROWS * (t + 1), :] = jnp.concatenate(pair, axis=0).astype(BF16)

    low_lanes = lax.broadcasted_iota(jnp.int32, (8, 128), 1) < 64
    low_wide = lax.broadcasted_iota(jnp.int32, (ROWS, 128), 1) < 64

    for h in range(2):
        mixed = jnp.dot(lat_t[LAT // 2 * h : LAT // 2 * (h + 1), :], weighted[...], preferred_element_type=F32)
        high = mixed.astype(BF16)
        both = jnp.concatenate([high, (mixed - high.astype(F32)).astype(BF16)], axis=0)
        both = jnp.dot(both, v_lonk[...], preferred_element_type=F32)
        grad = both[: LAT // 2] + both[LAT // 2 :]
        for i in range(8):
            for pair_at in range(2):
                t0, t1, t2 = (
                    grad[ROWS * i : ROWS * (i + 1), 384 * pair_at + 128 * j : 384 * pair_at + 128 * (j + 1)]
                    for j in range(3)
                )
                r1, r2 = pltpu.roll(t1, 64, 1), pltpu.roll(t2, 64, 1)
                for odd, (main, low, high) in enumerate(
                    ((t0, t1, r1), (jnp.where(low_wide, r1, r2), r2, t2))
                ):
                    eight = jnp.where(low_lanes, low[0:8], high[8:16])
                    four = jnp.where(low_lanes, low[16:24], pltpu.roll(high[16:24], 4, 0))
                    gsend[(8 * h + i) * 4 + 2 * pair_at + odd] = jnp.concatenate(
                        [main, eight, four[0:4]], axis=0
                    ).astype(BF16)

        def send_g(s, carry):
            to_lat = 8 * h + lax.rem(z + s // 4, 8)
            to_lon = lax.rem(lon + s, 4)
            to = to_lat * 4 + to_lon

            @pl.when(to != me)
            def _():
                remote(
                    gsend.at[to], grecv.at[me], g_send, g_recv.at[lat], {"lat": to_lat, "lon": to_lon}
                ).start()

            return carry

        lax.fori_loop(0, 32, send_g, 0)

    own_g = pltpu.make_async_copy(gsend.at[me], grecv.at[me], own_sem.at[2])
    own_g.start()
    own_g.wait()

    def take(s, carry):
        at = lax.rem(lat + s, 16)

        @pl.when(s == 0)
        def _():
            remote(grecv.at[pl.ds(0, 3)], grecv.at[pl.ds(0, 3)], g_send, g_recv.at[at], mate).wait_recv()

        @pl.when(s != 0)
        def _():
            remote(grecv.at[pl.ds(0, 4)], grecv.at[pl.ds(0, 4)], g_send, g_recv.at[at], mate).wait_recv()

        for k in range(LEVELS):
            out[at, k] = unpack(grecv[at * 4 + k].astype(F32)).astype(BF16)
        return carry

    lax.fori_loop(0, 16, take, 0)

    some = gsend.at[pl.ds(0, GROUP - 1)]
    remote(some, some, g_send, p_sem.at[1], mate).wait_send()
    for wait in sent:
        wait()


def shards(anomalies, innovation, corner_frac, corner_cell, cell_owner, latitude_kernel, longitude_kernel):
    dma = pltpu.SemaphoreType.DMA
    return pl.pallas_call(
        kernel,
        out_shape=pltpu.VMEM(anomalies.shape, BF16),
        in_specs=[pl.BlockSpec(memory_space=pltpu.HBM)] * 7,
        out_specs=pl.BlockSpec(memory_space=pltpu.VMEM),
        scratch_shapes=[
            pltpu.VMEM((1, OBS), F32),
            pltpu.VMEM((2, OBS), F32),
            pltpu.VMEM((1, OBS), jnp.int32),
            pltpu.VMEM((1, OBS), jnp.int32),
            pltpu.VMEM((LAT, LAT), BF16),
            pltpu.VMEM((LON, LON), BF16),
            pltpu.VMEM((2, 8, OBS), F32),
            pltpu.VMEM((2, LAT, CHUNK), BF16),
            pltpu.VMEM((2, HALF, CHUNK), BF16),
            pltpu.VMEM((LAT, HALF), F32),
            pltpu.VMEM((PLANE, ROWS, HALF), BF16),
            pltpu.VMEM((PLANE, ROWS, HALF), BF16),
            pltpu.VMEM((ROWS, HALF), BF16),
            pltpu.VMEM((DEPTH, ROWS, HALF), BF16),
            pltpu.VMEM((2, PLANE, ROWS, HALF), BF16),
            pltpu.VMEM((16, LEVELS, ROWS, COLS), BF16),
            pltpu.VMEM((DEPTH, 2, LEVELS, PACKED, 128), BF16),
            pltpu.VMEM((DEPTH, 2, LEVELS, PACKED, 128), BF16),
            pltpu.VMEM((8, DEPTH, PACKED, 128), BF16),
            pltpu.VMEM((LAT, LAT), BF16),
            pltpu.VMEM((LAT, LON), BF16),
            pltpu.VMEM((GROUP, PACKED, 128), BF16),
            pltpu.VMEM((GROUP, PACKED, 128), BF16),
            dma((7,)),
            dma((3,)),
            dma((2,)),
            dma((2,)),
            dma((2,)),
            dma((2, 2)),
            dma((2, 2)),
            dma((2,)),
            dma((2,)),
            dma,
            dma((16,)),
        ],
        compiler_params=pltpu.CompilerParams(
            collective_id=0, has_side_effects=True, vmem_limit_bytes=60 * 2**20
        ),
    )(*(
        pltpu.with_memory_space_constraint(x, pltpu.HBM)
        for x in (
            anomalies,
            innovation.reshape(1, OBS),
            corner_frac,
            corner_cell.reshape(1, OBS),
            cell_owner.reshape(1, OBS),
            latitude_kernel,
            longitude_kernel,
        )
    ))


def solution(mesh):
    placed = (
        P("mem", None, "lat", "lon"),
        P(("mem", "lat", "lon")),
        P(None, ("mem", "lat", "lon")),
        P(("mem", "lat", "lon")),
        P(("mem", "lat", "lon")),
        P(),
        P(),
    )
    return jax.shard_map(
        shards, mesh=mesh, in_specs=placed, out_specs=P("mem", None, "lat", "lon"), check_vma=False
    )
```

time: 70.3 us -> 58 us (0.83); the launches traced: 69.5 us -> 57.9 us
  local copies, waits for them, and re-layouts: 7.15 us -> 0.88 us
  Pallas kernels: 62.3 us -> 57 us
    unnamed x15 -> x1, local copies, waits for them, and re-layouts: 7.15 us -> 0.88 us
    pallas_call x1, Pallas kernels: 62.3 us -> 57 us  [shards(): pl.pallas_call(kernel, out_shape=pltpu.VMEM(anomalies.shape, BF16), in_sp...]
where the time goes in v2:
time: 58 us; the launch traced here: 57.9 us
  Pallas kernels  57 us (98%)
  local copies, waits for them, and re-layouts  0.88 us (2%)
    pallas_call x1, Pallas kernels, shards(): pl.pallas_call(kernel, out_shape=pltpu.VMEM(anomalies.shape, BF16), in_sp...  57 us

profile of v2, /device:TPU:16, one launch (start us, length us, event | category | flops | bytes accessed | tf_op | source)
XLA Modules:
  0.0 57.9 jit_solution(2593176109265186902)
XLA Ops:
  0.0 57.0 %shard_map.73 = bf16[16,4,24,192]{3,2,1,0:T(8,128)(2,1)S(1)} custom-call(bf16[16,4,24,192]{3,2,1,0:T(8,128)(2,1)} %anom.1, f32[1,4096]{1,0:T(1,128)} %bitcast.3, f32[2,4096]{1,0:T(2,128)} %frac.1, s32[1,4096]{1,0:T(1,128)} %bitcast.4, s32[1,4096]{1,0:T(1,128)} %bitcast.5, bf16[384,384]{1,0:T(8,128)(2,1)} %lat_k.1, bf16[768,768]{1,0:T(8,128)(2,1)} %lon_k.1), custom_call_target="tpu_custom_call" | custom-call | tf_op jit(solution)/shard_map/pallas_call | solution.py:335
  57.0 0.9 %copy.9 = bf16[16,4,24,192]{3,2,1,0:T(8,128)(2,1)} copy(bf16[16,4,24,192]{3,2,1,0:T(8,128)(2,1)S(1)} %shard_map.73) | data formatting | bytes 1179648

commit v3 on v2

--- a/solution.py
+++ b/solution.py
@@ -40,11 +40,11 @@
 def kernel(
     anom, innov, frac, cell, owner, lat_k, lon_k, out,
     v_innov, v_frac, v_cell, v_owner, v_latk, v_lonk,
-    obs, row_table, col_table, total,
+    obs, row_table, col_table, total, hsend, hrecv,
     psend, precv, zsend, zrecv, forcing,
     v_anom, fsend, frecv, field, lat_t, weighted, gsend, grecv,
     load_sem, own_sem,
-    obs_sem, p_sem, z_sem, f_sem, x_sem, ag_sem, core_sem, g_send, g_recv,
+    h_sem, p_sem, z_sem, f_sem, x_sem, ag_sem, core_sem, g_send, g_recv,
 ):
     mem, lat, lon = lax.axis_index("mem"), lax.axis_index("lat"), lax.axis_index("lon")
     core, y_lo = lax.rem(mem, 2), mem // 2
@@ -104,31 +104,25 @@
     cell_col = cells - cell_row * COLS
     tile = v_owner[...]
     value, a, b = v_innov[...], v_frac[0:1, :], v_frac[1:2, :]
-    obs[0, 0:1, :] = ((tile >> 2) * ROWS + cell_row).astype(F32)
-    obs[0, 1:2, :] = ((tile & 3) * COLS + cell_col).astype(F32)
-    obs[0, 2:3, :] = value * (1.0 - a)
-    obs[0, 3:4, :] = value * a
-    obs[0, 4:5, :] = 1.0 - b
-    obs[0, 5:6, :] = b
-    obs[0, 6:8, :] = jnp.zeros((2, OBS), F32)
-
-    first_col = (core * HALF).astype(F32)
-
-    def tables(slot, start):
-        at, use = pl.ds(start, CHUNK), (2 * slot + start // CHUNK) % 2
-        row_table[use] = tent_table(obs[slot, 0:1, at], obs[slot, 2:3, at], obs[slot, 3:4, at], LAT)
-        col_table[use] = tent_table(obs[slot, 1:2, at] - first_col, obs[slot, 4:5, at], obs[slot, 5:6, at], HALF)
-
-    def spread(part):
-        product = lax.dot_general(
-            row_table[part % 2], col_table[part % 2], (((1,), (1,)), ((), ())), preferred_element_type=F32
+    obs[0:1, :] = ((tile >> 2) * ROWS + cell_row).astype(F32)
+    obs[1:2, :] = ((tile & 3) * COLS + cell_col).astype(F32)
+    obs[2:3, :] = value * (1.0 - a)
+    obs[3:4, :] = value * a
+    obs[4:5, :] = 1.0 - b
+    obs[5:6, :] = b
+
+    def rows_of(part):
+        at = pl.ds(part * CHUNK, CHUNK)
+        row_table[part] = tent_table(obs[0:1, at], obs[2:3, at], obs[3:4, at], LAT)
+
+    def cols_of(part, half, use):
+        at, first = pl.ds(part * CHUNK, CHUNK), (half * HALF).astype(F32)
+        col_table[use] = tent_table(obs[1:2, at] - first, obs[4:5, at], obs[5:6, at], HALF)
+
+    def spread(part, use):
+        return lax.dot_general(
+            row_table[part], col_table[use], (((1,), (1,)), ((), ())), preferred_element_type=F32
         )
-        if part == 0:
-            total[...] = product
-        else:
-            total[...] += product
-
-    tables(0, 0)
 
     owed.pop(4)()
 
@@ -148,11 +142,20 @@
 
     lax.fori_loop(0, 16, pack, 0, unroll=2)
 
+    rows_of(0)
+    cols_of(0, 1 - core, 0)
+    total[...] = spread(0, 0)
+    rows_of(1)
+    cols_of(1, 1 - core, 1)
+    total[...] += spread(1, 1)
+    for p in range(PLANE):
+        hsend[p] = total[ROWS * p : ROWS * (p + 1), :].astype(BF16)
+
     pl.semaphore_wait(barrier, PLANE - 1 + DEPTH - 1 + 1)
-    obs_copy = remote(obs.at[0], obs.at[1], obs_sem.at[0], obs_sem.at[1], mate)
-    obs_copy.start()
-    owed["obs"] = obs_copy.wait_recv
-    sent.append(obs_copy.wait_send)
+    swap = remote(hsend, hrecv, h_sem.at[0], h_sem.at[1], mate)
+    swap.start()
+    owed["swap"] = swap.wait_recv
+    sent.append(swap.wait_send)
 
     offs = (4, 3, -3, 2, -2, 1, -1)
 
@@ -167,17 +170,14 @@
     own_f.start()
     owed["own_f"] = own_f.wait
 
-    spread(0)
-    tables(0, CHUNK)
-    owed.pop("obs")()
-    spread(1)
-    tables(1, 0)
-    spread(2)
-    tables(1, CHUNK)
-    spread(3)
+    cols_of(0, core, 2)
+    total[...] = spread(0, 2)
+    cols_of(1, core, 3)
+    total[...] += spread(1, 3)
+    owed.pop("swap")()
 
     for p in range(PLANE):
-        psend[p] = total[ROWS * p : ROWS * (p + 1), :].astype(BF16)
+        psend[p] = (total[ROWS * p : ROWS * (p + 1), :] + hrecv[p].astype(F32)).astype(BF16)
 
     def send_p(s, carry):
         to = lax.rem(q + s, PLANE)
@@ -191,7 +191,7 @@
     lat_t[...] = v_latk[...].astype(F32).T.astype(BF16)
 
     owed.pop("p")()
-    band = total[pl.ds(pl.multiple_of(q * ROWS, 8), ROWS), :]
+    band = total[pl.ds(pl.multiple_of(q * ROWS, 8), ROWS), :] + hrecv[q].astype(F32)
     for s in range(1, PLANE):
         band = band + precv[lax.rem(q + s, PLANE)].astype(F32)
 
@@ -266,13 +266,13 @@
     low_lanes = lax.broadcasted_iota(jnp.int32, (8, 128), 1) < 64
     low_wide = lax.broadcasted_iota(jnp.int32, (ROWS, 128), 1) < 64
 
-    for h in range(2):
-        mixed = jnp.dot(lat_t[LAT // 2 * h : LAT // 2 * (h + 1), :], weighted[...], preferred_element_type=F32)
+    for h in range(4):
+        mixed = jnp.dot(lat_t[LAT // 4 * h : LAT // 4 * (h + 1), :], weighted[...], preferred_element_type=F32)
         high = mixed.astype(BF16)
         both = jnp.concatenate([high, (mixed - high.astype(F32)).astype(BF16)], axis=0)
         both = jnp.dot(both, v_lonk[...], preferred_element_type=F32)
-        grad = both[: LAT // 2] + both[LAT // 2 :]
-        for i in range(8):
+        grad = both[: LAT // 4] + both[LAT // 4 :]
+        for i in range(4):
             for pair_at in range(2):
                 t0, t1, t2 = (
                     grad[ROWS * i : ROWS * (i + 1), 384 * pair_at + 128 * j : 384 * pair_at + 128 * (j + 1)]
@@ -284,12 +284,12 @@
                 ):
                     eight = jnp.where(low_lanes, low[0:8], high[8:16])
                     four = jnp.where(low_lanes, low[16:24], pltpu.roll(high[16:24], 4, 0))
-                    gsend[(8 * h + i) * 4 + 2 * pair_at + odd] = jnp.concatenate(
+                    gsend[(4 * h + i) * 4 + 2 * pair_at + odd] = jnp.concatenate(
                         [main, eight, four[0:4]], axis=0
                     ).astype(BF16)
 
         def send_g(s, carry):
-            to_lat = 8 * h + lax.rem(z + s // 4, 8)
+            to_lat = 4 * h + lax.rem(z + s // 4, 4)
             to_lon = lax.rem(lon + s, 4)
             to = to_lat * 4 + to_lon
 
@@ -301,7 +301,7 @@
 
             return carry
 
-        lax.fori_loop(0, 32, send_g, 0)
+        lax.fori_loop(0, 16, send_g, 0)
 
     own_g = pltpu.make_async_copy(gsend.at[me], grecv.at[me], own_sem.at[2])
     own_g.start()
@@ -344,10 +344,12 @@
             pltpu.VMEM((1, OBS), jnp.int32),
             pltpu.VMEM((LAT, LAT), BF16),
             pltpu.VMEM((LON, LON), BF16),
-            pltpu.VMEM((2, 8, OBS), F32),
+            pltpu.VMEM((8, OBS), F32),
             pltpu.VMEM((2, LAT, CHUNK), BF16),
-            pltpu.VMEM((2, HALF, CHUNK), BF16),
+            pltpu.VMEM((4, HALF, CHUNK), BF16),
             pltpu.VMEM((LAT, HALF), F32),
+            pltpu.VMEM((PLANE, ROWS, HALF), BF16),
+            pltpu.VMEM((PLANE, ROWS, HALF), BF16),
             pltpu.VMEM((PLANE, ROWS, HALF), BF16),
             pltpu.VMEM((PLANE, ROWS, HALF), BF16),
             pltpu.VMEM((ROWS, HALF), BF16),

time: 58 us -> 53.8 us (0.928)
  Pallas kernels: 57 us -> 52.5 us
    pallas_call x1, Pallas kernels: 57 us -> 52.5 us  [shards(): pl.pallas_call(kernel, out_shape=pltpu.VMEM(anomalies.shape, BF16), in_sp...]
where the time goes in v3:
time: 53.8 us; the launch traced here: 53.4 us
  Pallas kernels  52.5 us (98%)
  local copies, waits for them, and re-layouts  0.88 us (2%)
    pallas_call x1, Pallas kernels, shards(): pl.pallas_call(kernel, out_shape=pltpu.VMEM(anomalies.shape, BF16), in_sp...  52.5 us

profile of v3, /device:TPU:16, one launch (start us, length us, event | category | flops | bytes accessed | tf_op | source)
XLA Modules:
  0.0 53.4 jit_solution(6049088817028015660)
XLA Ops:
  0.0 52.5 %shard_map.73 = bf16[16,4,24,192]{3,2,1,0:T(8,128)(2,1)S(1)} custom-call(bf16[16,4,24,192]{3,2,1,0:T(8,128)(2,1)} %anom.1, f32[1,4096]{1,0:T(1,128)} %bitcast.3, f32[2,4096]{1,0:T(2,128)} %frac.1, s32[1,4096]{1,0:T(1,128)} %bitcast.4, s32[1,4096]{1,0:T(1,128)} %bitcast.5, bf16[384,384]{1,0:T(8,128)(2,1)} %lat_k.1, bf16[768,768]{1,0:T(8,128)(2,1)} %lon_k.1), custom_call_target="tpu_custom_call" | custom-call | tf_op jit(solution)/shard_map/pallas_call | solution.py:335
  52.5 0.9 %copy.9 = bf16[16,4,24,192]{3,2,1,0:T(8,128)(2,1)} copy(bf16[16,4,24,192]{3,2,1,0:T(8,128)(2,1)S(1)} %shard_map.73) | data formatting | bytes 1179648

commit v4 on v3

--- a/solution.py
+++ b/solution.py
@@ -15,7 +15,7 @@
 LAT, LON, OBS = 384, 768, 4096
 HALF = LON // 2
 PLANE, DEPTH, GROUP = 16, 8, 64
-CHUNK = 2048
+CHUNK = 4096
 PACKED = 36
 
 
@@ -144,12 +144,9 @@
 
     rows_of(0)
     cols_of(0, 1 - core, 0)
-    total[...] = spread(0, 0)
-    rows_of(1)
-    cols_of(1, 1 - core, 1)
-    total[...] += spread(1, 1)
+    other = spread(0, 0)
     for p in range(PLANE):
-        hsend[p] = total[ROWS * p : ROWS * (p + 1), :].astype(BF16)
+        hsend[p] = other[ROWS * p : ROWS * (p + 1), :].astype(BF16)
 
     pl.semaphore_wait(barrier, PLANE - 1 + DEPTH - 1 + 1)
     swap = remote(hsend, hrecv, h_sem.at[0], h_sem.at[1], mate)
@@ -170,10 +167,8 @@
     own_f.start()
     owed["own_f"] = own_f.wait
 
-    cols_of(0, core, 2)
-    total[...] = spread(0, 2)
-    cols_of(1, core, 3)
-    total[...] += spread(1, 3)
+    cols_of(0, core, 1)
+    total[...] = spread(0, 1)
     owed.pop("swap")()
 
     for p in range(PLANE):
@@ -345,8 +340,8 @@
             pltpu.VMEM((LAT, LAT), BF16),
             pltpu.VMEM((LON, LON), BF16),
             pltpu.VMEM((8, OBS), F32),
-            pltpu.VMEM((2, LAT, CHUNK), BF16),
-            pltpu.VMEM((4, HALF, CHUNK), BF16),
+            pltpu.VMEM((1, LAT, CHUNK), BF16),
+            pltpu.VMEM((2, HALF, CHUNK), BF16),
             pltpu.VMEM((LAT, HALF), F32),
             pltpu.VMEM((PLANE, ROWS, HALF), BF16),
             pltpu.VMEM((PLANE, ROWS, HALF), BF16),

time: 53.8 us -> 53.7 us (level)
  no operation moved by 1% of the time
where the time goes in v4:
time: 53.7 us; the launch traced here: 53 us
  Pallas kernels  52.1 us (97%)
  local copies, waits for them, and re-layouts  0.88 us (2%)
    pallas_call x1, Pallas kernels, shards(): pl.pallas_call(kernel, out_shape=pltpu.VMEM(anomalies.shape, BF16), in_sp...  52.1 us

profile of v4, /device:TPU:16, one launch (start us, length us, event | category | flops | bytes accessed | tf_op | source)
XLA Modules:
  0.0 53.0 jit_solution(249674784379006505)
XLA Ops:
  0.0 52.1 %shard_map.73 = bf16[16,4,24,192]{3,2,1,0:T(8,128)(2,1)S(1)} custom-call(bf16[16,4,24,192]{3,2,1,0:T(8,128)(2,1)} %anom.1, f32[1,4096]{1,0:T(1,128)} %bitcast.3, f32[2,4096]{1,0:T(2,128)} %frac.1, s32[1,4096]{1,0:T(1,128)} %bitcast.4, s32[1,4096]{1,0:T(1,128)} %bitcast.5, bf16[384,384]{1,0:T(8,128)(2,1)} %lat_k.1, bf16[768,768]{1,0:T(8,128)(2,1)} %lon_k.1), custom_call_target="tpu_custom_call" | custom-call | tf_op jit(solution)/shard_map/pallas_call | solution.py:330
  52.1 0.9 %copy.9 = bf16[16,4,24,192]{3,2,1,0:T(8,128)(2,1)} copy(bf16[16,4,24,192]{3,2,1,0:T(8,128)(2,1)S(1)} %shard_map.73) | data formatting | bytes 1179648

commit v5 on v4

--- a/solution.py
+++ b/solution.py
@@ -58,6 +58,10 @@
         y = p // 4
         return {"mem": lax.rem(y, 2) * 2 + core, "lat": (y // 2) * 8 + z, "lon": lax.rem(p, 4)}
 
+    def far_first(s):
+        s = s - 1 + s // 11
+        return lax.rem(q // 4 + 2 + s // 4, 4) * 4 + lax.rem(lon + 2 + s, 4)
+
     def z_peer(to):
         return {"lat": y_hi * 8 + to}
 
@@ -175,7 +179,7 @@
         psend[p] = (total[ROWS * p : ROWS * (p + 1), :] + hrecv[p].astype(F32)).astype(BF16)
 
     def send_p(s, carry):
-        to = lax.rem(q + s, PLANE)
+        to = far_first(s)
         remote(psend.at[to], precv.at[q], p_sem.at[0], p_sem.at[1], plane_peer(to)).start()
         return carry
 
@@ -225,7 +229,7 @@
     forcing[core, q] = band.astype(BF16)
 
     def send_ag(s, carry):
-        to = lax.rem(q + s, PLANE)
+        to = far_first(s)
         remote(forcing.at[core, q], forcing.at[core, q], ag_sem.at[0], ag_sem.at[1], plane_peer(to)).start()
         return carry
 

time: 53.7 us -> 53.9 us (level)
  no operation moved by 1% of the time
where the time goes in v5:
time: 53.9 us; the launch traced here: 53.3 us
  Pallas kernels  52.4 us (97%)
  local copies, waits for them, and re-layouts  0.88 us (2%)
    pallas_call x1, Pallas kernels, shards(): pl.pallas_call(kernel, out_shape=pltpu.VMEM(anomalies.shape, BF16), in_sp...  52.4 us

profile of v5, /device:TPU:16, one launch (start us, length us, event | category | flops | bytes accessed | tf_op | source)
XLA Modules:
  0.0 53.3 jit_solution(11360552559009048612)
XLA Ops:
  0.0 52.4 %shard_map.73 = bf16[16,4,24,192]{3,2,1,0:T(8,128)(2,1)S(1)} custom-call(bf16[16,4,24,192]{3,2,1,0:T(8,128)(2,1)} %anom.1, f32[1,4096]{1,0:T(1,128)} %bitcast.3, f32[2,4096]{1,0:T(2,128)} %frac.1, s32[1,4096]{1,0:T(1,128)} %bitcast.4, s32[1,4096]{1,0:T(1,128)} %bitcast.5, bf16[384,384]{1,0:T(8,128)(2,1)} %lat_k.1, bf16[768,768]{1,0:T(8,128)(2,1)} %lon_k.1), custom_call_target="tpu_custom_call" | custom-call | tf_op jit(solution)/shard_map/pallas_call | solution.py:334
  52.4 0.9 %copy.9 = bf16[16,4,24,192]{3,2,1,0:T(8,128)(2,1)} copy(bf16[16,4,24,192]{3,2,1,0:T(8,128)(2,1)S(1)} %shard_map.73) | data formatting | bytes 1179648
